TPU v7x, 256 devices: a whole 4x4x8 slice. The times are simulated.
256 devices in a mesh: sec: 16 (over z, core), env: 16 (over y, x).
Axes of the slice: x: 4, y: 4, z: 8, core: 2. Of those that a mesh axis runs over, the one named last changes fastest.
Arguments:
- env_left: bfloat16 [32, 40, 128, 128], P('sec', None, 'env'), may hold values from -6 to 6
- env_right: bfloat16 [32, 40, 128, 128], P('sec', None, 'env'), may hold values from -6 to 6
- site_left: bfloat16 [2048, 128, 128], P('sec'), may hold values from -0.25 to 0.25
- site_right: bfloat16 [2048, 128, 128], P('sec'), may hold values from -0.25 to 0.25
- source_left: int32 [2048], P('sec'), may hold values from 0 to 31, as said below
- source_right: int32 [2048], P('sec'), may hold values from 0 to 31, as said below
- channel_left: int32 [2048], P('sec'), may hold values from 0 to 7
- channel_right: int32 [2048], P('sec'), may hold values from 0 to 7
- fanin_left: int32 [32], P('sec'), may hold values from 8 to 64, as said below
- fanin_right: int32 [32], P('sec'), may hold values from 8 to 64, as said below
- operator_table: bfloat16 [8, 40, 40], replicated, may hold values from -1.25 to 1.25
- operator_pattern: int32 [8, 40, 40], replicated, may hold values 0 or 1
Outputs:
- new_left: bfloat16 [32, 40, 128, 128], P('sec', None, 'env')
- new_right: bfloat16 [32, 40, 128, 128], P('sec', None, 'env')
Inputs may be any that keep to these rules, and one draw needn't show every extreme that they name: `source_left`: among the 128 slots held by one index of sec, all sources owned by one index q of sec (sectors 2 * q to 2 * q + 1) are one and the same sector. `source_right`: among the 128 slots held by one index of sec, all sources owned by one index q of sec are one and the same sector. `fanin_left`: some sector has all 64 slots live. `fanin_right`: some sector has all 64 slots live.
All inputs are finite; a program needn't handle non-finite values.
Results may differ from a plain program's by a relative error of at most 0.015.
Values may be sent and summed in bfloat16 or wider, within the bound.
A program may use at most 128 MiB of HBM per device.

v0:
```python
import jax
import jax.numpy as jnp
from jax import lax
from jax.sharding import PartitionSpec as P


def fetch_tiles(old_tiles, source):
    everything = lax.all_gather(old_tiles, "sec", axis=0, tiled=True)
    return jnp.take(everything, source, axis=0)


def contract(fetched, blocks, mix_slots, rows_here):
    sec_dev, group, channels, row_count, states = fetched.shape
    batch = sec_dev * group
    tiles_flat = fetched.reshape(batch, channels * row_count, states)
    blocks_flat = blocks.reshape(batch, states, states)
    first_section = lax.dot_general(
        tiles_flat, blocks_flat, (((2,), (1,)), ((0,), (0,))), preferred_element_type=jnp.float32
    ).astype(jnp.bfloat16)
    first_section = first_section.reshape(batch, channels, row_count * states)
    mix_flat = mix_slots.reshape(batch, channels, channels)
    mixed_section = lax.dot_general(
        mix_flat, first_section, (((1,), (1,)), ((0,), (0,))), preferred_element_type=jnp.float32
    ).astype(jnp.bfloat16)
    mixed_section = mixed_section.reshape(sec_dev, group, channels, row_count, states)
    mixed_rows = jnp.transpose(mixed_section, (0, 1, 3, 2, 4)).reshape(
        sec_dev, group * row_count, channels * states
    )
    rows_flat = rows_here.reshape(sec_dev, group * row_count, states)
    partial_value = lax.dot_general(
        rows_flat, mixed_rows, (((1,), (1,)), ((0,), (0,))), preferred_element_type=jnp.float32
    )
    partial_value = partial_value.reshape(sec_dev, states, channels, states)
    return jnp.transpose(partial_value, (0, 2, 1, 3))


def rebuild(old_tiles, site_blocks, source, channel, fan_in, mixing):
    sec_dev, channels, row_count, states = old_tiles.shape
    slot_count = site_blocks.shape[0]
    per_sector = slot_count // sec_dev
    live_grid = jnp.arange(per_sector, dtype=jnp.int32)[None, :] < fan_in[:, None]
    live_slots = live_grid.reshape(slot_count)
    blocks = jnp.where(live_slots[:, None, None], site_blocks, jnp.zeros_like(site_blocks))
    blocks = blocks.reshape(sec_dev, per_sector, states, states)
    fetched = fetch_tiles(old_tiles, source).reshape(
        sec_dev, per_sector, channels, row_count, states
    )
    op_count = mixing.shape[0]
    one_hot = (channel[:, None] == jnp.arange(op_count, dtype=jnp.int32)[None, :]).astype(
        jnp.bfloat16
    )
    mix_slots = jnp.dot(
        one_hot, mixing.reshape(op_count, channels * channels), preferred_element_type=jnp.float32
    )
    mix_slots = mix_slots.astype(jnp.bfloat16).reshape(sec_dev, per_sector, channels, channels)
    row_start = lax.axis_index("env") * row_count
    rows_here = lax.dynamic_slice_in_dim(blocks, row_start, row_count, 2)
    partial_value = contract(fetched, blocks, mix_slots, rows_here)
    rounded = partial_value.astype(jnp.bfloat16)
    return (
        lax.psum_scatter(rounded, "env", scatter_dimension=2, tiled=True)
        .astype(jnp.float32)
        .astype(jnp.bfloat16)
    )


def per_device(
    env_left,
    env_right,
    site_left,
    site_right,
    source_left,
    source_right,
    channel_left,
    channel_right,
    fanin_left,
    fanin_right,
    operator_table,
    operator_pattern,
):
    operator = operator_table * operator_pattern.astype(operator_table.dtype)
    new_left = rebuild(env_left, site_left, source_left, channel_left, fanin_left, operator)
    new_right = rebuild(
        env_right,
        site_right,
        source_right,
        channel_right,
        fanin_right,
        jnp.transpose(operator, (0, 2, 1)),
    )
    return (new_left, new_right)


def solution(mesh):
    in_specs = (
        P("sec", None, "env", None),
        P("sec", None, "env", None),
        P("sec", None, None),
        P("sec", None, None),
        P("sec"),
        P("sec"),
        P("sec"),
        P("sec"),
        P("sec"),
        P("sec"),
        P(),
        P(),
    )
    out_specs = (P("sec", None, "env", None), P("sec", None, "env", None))
    return jax.shard_map(
        per_device, mesh=mesh, in_specs=in_specs, out_specs=out_specs, check_vma=False
    )
```

profile of v0, /device:TPU:1, one launch (start us, length us, event | category | flops | bytes accessed | tf_op | source)
XLA Modules:
  0.0 313.3 jit_solution(12414070120489753704)
XLA Ops:
  7.2 0.0 copy-start.1
  7.2 0.0 copy-start.2
  7.2 0.0 all-gather.5.cloned.1.call-start
  7.2 0.7 all-gather.5.cloned.1.call-update
  7.9 0.0 all-gather.3.cloned.1.call-start
  8.0 0.7 all-gather.3.cloned.1.call-update
  8.7 0.0 all-reduce.5.cloned.1.call-start
  8.7 0.7 iota_compare_fusion.4
  9.4 0.1 lt.58
  9.5 0.7 compare_select_fusion
  10.2 1.0 convert_multiply_fusion
  11.2 0.1 reshape.83
  11.3 0.1 copy.30
  11.4 0.1 reshape.89
  11.5 1.0 convolution_convert_fusion.2
  12.6 1.2 copy.31
  13.8 0.7 iota_compare_fusion.5
  14.5 0.1 lt.53
  14.6 0.7 compare_select_fusion.1
  15.3 1.0 convolution_convert_fusion.3
  16.3 1.2 copy.27
  17.5 0.0 copy-start
  17.6 0.0 copy-done.1
  17.6 0.0 copy-done.2
  17.6 4.7 %broadcast_select_fusion = bf16[128,128,128]{2,1,0:T(8,128)(2,1)} fusion(bf16[128,128,128]{2,1,0:T(8,128)(2,1)} %param.17, pred[128]{0:T(512)(128)(4,1)S(1)} %lt.58), kind=kLoop, calls=%fused_computation.22 | loop fusion | flops 2097152 | bytes 8388736 | tf_op jit(solution)/shard_map/jit(_where)/select_n | solution.py:43
  22.3 0.0 copy-done
  22.3 2.3 broadcast_select_fusion.1
  24.6 29.8 %all-gather.5.cloned.1.call-done = bf16[32,40,8,128]{3,2,1,0:T(8,128)(2,1)} async-done(((bf16[2,40,8,128]{3,2,1,0:T(8,128)(2,1)}), bf16[32,40,8,128]{3,2,1,0:T(8,128)(2,1)}) %all-gather.5.cloned.1.call-update) | async-done | bytes 2621456 | tf_op jit(solution)/shard_map/all_gather | solution.py:8
  54.5 9.3 %gather_fusion.1 = bf16[128,40,8,128]{3,2,1,0:T(8,128)(2,1)} fusion(bf16[32,40,8,128]{3,2,1,0:T(8,128)(2,1)} %all-gather.5.cloned.1.call-done, s32[1024]{0:T(1024)S(1)} %pad_clamp_fusion), kind=kCustom, calls=%fused_computation.1.clone | custom fusion | bytes 20972032 | tf_op jit(solution)/shard_map/jit(_take)/gather | solution.py:9
  63.8 9.5 %fusion.15 = bf16[128,320,128]{2,1,0:T(8,128)(2,1)} fusion(bf16[128,128,128]{2,1,0:T(8,128)(2,1)} %broadcast_select_fusion, bf16[128,40,8,128]{3,2,1,0:T(8,128)(2,1)} %gather_fusion.1, pred[128]{0:T(512)(128)(4,1)S(1)} %compare_and_fusion), kind=kOutput, calls=%fused_computation.17 | convolution fusion | flops 1352663040 | bytes 25165952 | tf_op jit(solution)/shard_map/dot_general | solution.py:17
  73.3 16.4 %reshape.90 = bf16[128,40,1024]{2,1,0:T(8,128)(2,1)} reshape(bf16[128,320,128]{2,1,0:T(8,128)(2,1)} %fusion.15) | data formatting | bytes 20971520 | tf_op jit(solution)/shard_map/reshape | solution.py:20
  89.8 10.7 %convolution_convert_fusion = bf16[128,40,1024]{2,1,0:T(8,128)(2,1)} fusion(bf16[128,40,40]{1,2,0:T(8,128)(2,1)S(1)} %copy.31, bf16[128,40,1024]{2,1,0:T(8,128)(2,1)} %reshape.90), kind=kOutput, calls=%fused_computation.14 | convolution fusion | flops 424673280 | bytes 21381120 | tf_op jit(solution)/shard_map/dot_general | solution.py:22
  100.4 10.7 %copy.43 = bf16[640,8,8,128]{3,2,1,0:T(8,128)(2,1)} copy(bf16[640,8,8,128]{3,1,2,0:T(8,128)(2,1)} %bitcast.77) | data formatting | bytes 20971520
  111.1 5.8 %fusion.26 = bf16[2,16,40,8,128]{4,3,2,1,0:T(8,128)(2,1)S(1)} fusion(bf16[2,64,40,8,128]{4,3,2,1,0:T(8,128)(2,1)} %bitcast.78, bf16[2,64,128,128]{3,2,1,0:T(8,128)(2,1)} %bitcast.83, s32[]{:T(128)S(6)} %select_n.19), kind=kOutput, calls=%fused_computation.28 | convolution fusion | flops 1343488000 | bytes 13369348 | tf_op jit(solution)/shard_map/dot_general | solution.py:30
  116.9 2.3 copy.46
  119.2 0.0 all-gather.3.cloned.1.call-done
  119.2 9.3 %gather_fusion = bf16[128,40,8,128]{3,2,1,0:T(8,128)(2,1)} fusion(bf16[32,40,8,128]{3,2,1,0:T(8,128)(2,1)} %all-gather.3.cloned.1.call-done, s32[1024]{0:T(1024)S(1)} %pad_clamp_fusion.1), kind=kCustom, calls=%fused_computation.clone | custom fusion | bytes 20972032 | tf_op jit(solution)/shard_map/jit(_take)/gather | solution.py:9
  128.5 9.3 %fusion.12 = bf16[128,320,128]{2,1,0:T(8,128)(2,1)} fusion(bf16[128,128,128]{2,1,0:T(8,128)(2,1)} %broadcast_select_fusion.1, bf16[128,40,8,128]{3,2,1,0:T(8,128)(2,1)} %gather_fusion, pred[128]{0:T(512)(128)(4,1)S(1)} %compare_and_fusion.1), kind=kOutput, calls=%fused_computation.16 | convolution fusion | flops 1352663040 | bytes 25165952 | tf_op jit(solution)/shard_map/dot_general | solution.py:17
  137.8 16.3 %reshape.84 = bf16[128,40,1024]{2,1,0:T(8,128)(2,1)} reshape(bf16[128,320,128]{2,1,0:T(8,128)(2,1)} %fusion.12) | data formatting | bytes 20971520 | tf_op jit(solution)/shard_map/reshape | solution.py:20
  154.1 10.7 %convolution_convert_fusion.1 = bf16[128,40,1024]{2,1,0:T(8,128)(2,1)} fusion(bf16[128,40,40]{1,2,0:T(8,128)(2,1)S(1)} %copy.27, bf16[128,40,1024]{2,1,0:T(8,128)(2,1)} %reshape.84), kind=kOutput, calls=%fused_computation.15 | convolution fusion | flops 424673280 | bytes 21381120 | tf_op jit(solution)/shard_map/dot_general | solution.py:22
  164.8 10.7 %copy.42 = bf16[640,8,8,128]{3,2,1,0:T(8,128)(2,1)} copy(bf16[640,8,8,128]{3,1,2,0:T(8,128)(2,1)} %bitcast.79) | data formatting | bytes 20971520
  175.5 5.8 %fusion.29 = bf16[2,16,40,8,128]{4,3,2,1,0:T(8,128)(2,1)S(1)} fusion(bf16[2,64,40,8,128]{4,3,2,1,0:T(8,128)(2,1)} %bitcast.76, bf16[2,64,128,128]{3,2,1,0:T(8,128)(2,1)} %bitcast.82, s32[]{:T(128)S(6)} %select_n.19), kind=kOutput, calls=%fused_computation.29 | convolution fusion | flops 1343488000 | bytes 13369348 | tf_op jit(solution)/shard_map/dot_general | solution.py:30
  181.2 0.0 copy-start.3
  181.2 2.2 copy.47
  183.5 0.0 all-reduce.5.cloned.1.call-update
  183.5 0.0 copy-done.3
  183.5 0.6 dynamic-slice
  184.7 120.3 %all-reduce.5.cloned.1.call-done = (bf16[2,40,128,128]{3,2,1,0:T(8,128)(2,1)}, bf16[2,40,128,128]{3,2,1,0:T(8,128)(2,1)}) async-done(((bf16[2,40,128,128]{3,2,1,0:T(8,128)(2,1)}, bf16[2,40,128,128]{3,2,1,0:T(8,128)(2,1)}), (bf16[2,40,128,128]{3,2,1,0:T(8,128)(2,1)}, bf16[2,40,128,128]{3,2,1,0:T(8,128)(2,1)})) %all-reduce.5.cloned.1.call-update) | async-done | bytes 5242896
  305.0 1.7 constant_dynamic-slice_fusion
  (4 shorter events, 0.0 us)
Async XLA Ops:
  7.2 10.4 %copy-start.1 = (s32[128]{0:T(128)S(1)}, s32[128]{0:T(128)}, u32[]{:S(2)}) copy-start(s32[128]{0:T(128)} %param.19) | copy-start | bytes 1540
  7.2 10.4 %copy-start.2 = (s32[128]{0:T(128)S(1)}, s32[128]{0:T(128)}, u32[]{:S(2)}) copy-start(s32[128]{0:T(128)} %param.18) | copy-start | bytes 1540
  7.2 47.3 %all-gather.5.cloned.1.call-start = ((), (), s32[]{:S(2)}) async-start(), calls=%async_computation.1 | async-start | bytes 2785280 | tf_op jit(solution)/shard_map/all_gather | solution.py:8
  7.9 111.3 %all-gather.3.cloned.1.call-start = ((), (), s32[]{:S(2)}) async-start(), calls=%async_computation | async-start | bytes 2785280 | tf_op jit(solution)/shard_map/all_gather | solution.py:8
  8.7 296.3 %all-reduce.5.cloned.1.call-start = ((), (), s32[]{:S(2)}) async-start(), calls=%async_computation.2 | async-start | bytes 10485760
  17.5 4.8 %copy-start = (bf16[128,128,128]{2,1,0:T(8,128)(2,1)S(1)}, bf16[128,128,128]{2,1,0:T(8,128)(2,1)}, u32[]{:S(2)}) copy-start(bf16[128,128,128]{2,1,0:T(8,128)(2,1)} %param.16) | copy-start | bytes 12582916
  181.2 2.3 copy-start.3
Sparse Core Ops, SparseCore 0:
  9.9 44.5 all-gather.4
  56.3 38.8 all-gather.2
  183.6 121.3 all-reduce.4
where the time goes:
time: 315 us; the launch traced here: 313 us
  waiting for transfers between devices  152 us (48%)
  local copies, waits for them, and re-layouts  82.6 us (26%)
  matrix products  53.8 us (17%)
  between operations  14.6 us (5%)
  other arithmetic  10.8 us (3%)
    unnamed x4, waiting for transfers between devices  122 us
    reshape x2, local copies, waits for them, and re-layouts, contract(): first_section = first_section.reshape(batch, channels, row_count * states)  32.7 us
    all_gather x2, waiting for transfers between devices, fetch_tiles(): everything = lax.all_gather(old_tiles, 'sec', axis=0, tiled=True)  29.8 us
    unnamed x12, local copies, waits for them, and re-layouts  23.7 us
    dot_general x2, matrix products, contract(): lax.dot_general(mix_flat, first_section, (((1,), (1,)), ((0,), (0,))), pr...  21.4 us
    dot_general x2, matrix products, contract(): lax.dot_general(tiles_flat, blocks_flat, (((2,), (1,)), ((0,), (0,))), pr...  18.8 us
    gather x2, local copies, waits for them, and re-layouts, fetch_tiles(): return jnp.take(everything, source, axis=0)  18.6 us
    dot_general x2, matrix products, contract(): lax.dot_general(rows_flat, mixed_rows, (((1,), (1,)), ((0,), (0,))), pref...  11.5 us
  transfers between devices with their start and end apart: 3, of which 2 were waited for; matrix products, arithmetic and copies ran while one was open for 26% of the time, Pallas kernels for 0%

commit v1 on v0

v1 whole, which is shorter than its diff:
```python
import functools

import jax
import jax.numpy as jnp
from jax import lax
from jax.experimental import pallas as pl
from jax.experimental.pallas import tpu as pltpu
from jax.sharding import PartitionSpec as P

MESH = pl.DeviceIdType.MESH
BF, F32 = jnp.bfloat16, jnp.float32
NZ, NX, NY = 8, 4, 4
LAST = NZ - 2
W, R, S = 40, 8, 128
WR = W * R
HALF = WR // 2
SLOTS, CHANNELS = 64, 8


def dot(a, b):
    return lax.dot_general(a, b, (((1,), (0,)), ((), ())), preferred_element_type=F32)


def kernel(
    fan_l, fan_r, src_l, src_r, chn_l, chn_r, srcv_l, srcv_r, table, pattern, env_l, env_r, site_l, site_r,
    out_l, out_r,
    got, site, kron, mixenv, mixed, rows_t, send1, recv1, send2, recv2,
    loc_sem, ring_s, ring_r, cross_s, cross_r, s1_s, s1_r, s2_s, s2_r,
):
    fan, src, chn, srcv = (fan_l, fan_r), (src_l, src_r), (chn_l, chn_r), (srcv_l, srcv_r)
    env_in, site_in, out = (env_l, env_r), (site_l, site_r), (out_l, out_r)
    sec, env = lax.axis_index("sec"), lax.axis_index("env")
    z, core = sec // 2, sec % 2
    y, x = env // NX, env % NX
    other = (z * 2 + 1 - core, env)
    up = (lax.rem(z + 1, NZ) * 2 + core, env)
    down = (lax.rem(z + NZ - 1, NZ) * 2 + core, env)
    x_peer = [(sec, y * NX + lax.rem(x + d, NX)) for d in range(1, NX)]
    y_peer = [(sec, lax.rem(y + d, NY) * NX + x) for d in range(1, NY)]

    barrier = pltpu.get_barrier_semaphore()
    partners = [other, up, down] + x_peer + y_peer
    for peer in partners:
        pl.semaphore_signal(barrier, inc=1, device_id=peer, device_id_type=MESH)
    pl.semaphore_wait(barrier, len(partners))

    def remote(a, b, ssem, rsem, peer):
        return pltpu.make_async_remote_copy(
            src_ref=a, dst_ref=b, send_sem=ssem, recv_sem=rsem, device_id=peer, device_id_type=MESH
        )

    def chunk_of(way, n):
        far = n // 2 + 1
        chip = lax.rem(z + NZ - far, NZ) if way == 0 else lax.rem(z + far, NZ)
        h = n % 2 if n < LAST else way
        return chip, h

    def ring(side, way, n):
        peer = up if way == 0 else down
        if n < 2:
            a, chip, h = env_in[side].at[n], z, n
        else:
            back = n - 2 if (n < LAST or way == 0) else n - 1
            chip, h = chunk_of(way, back)
            a = got.at[side, chip * 2 + core, h]
        return remote(a, got.at[side, chip * 2 + core, h], ring_s.at[side, way, n], ring_r.at[side, way, n], peer)

    def ring_in(side, way, n):
        chip, h = chunk_of(way, n)
        spot = got.at[side, chip * 2 + core, h]
        return remote(spot, spot, ring_s.at[side, way, n], ring_r.at[side, way, n], up if way == 0 else down)

    def cross(side, way, n):
        if way == 2:
            a, chip, h, c = env_in[side].at[n], z, n, n
        else:
            chip, h = chunk_of(way, n)
            a, c = got.at[side, chip * 2 + core, h], 2 + 2 * n + way
        return remote(a, got.at[side, chip * 2 + core, h], cross_s.at[side, c], cross_r.at[side, c], other)

    def cross_in(side, way, n):
        chip, h, c = (z, n, n) if way == 2 else (*chunk_of(way, n), 2 + 2 * n + way)
        spot = got.at[side, chip * 2 + 1 - core, h]
        return remote(spot, spot, cross_s.at[side, c], cross_r.at[side, c], other)

    def gather_start(side):
        for n in range(2):
            ring(side, 0, n).start()
            ring(side, 1, n).start()
        for n in range(2):
            cross(side, 2, n).start()

    def gather_step(side, n):
        for way in range(2):
            ring_in(side, way, n).wait_recv()
            for later in range(2, LAST + 1):
                back = later - 2 if (later < LAST or way == 0) else later - 1
                if back == n:
                    ring(side, way, later).start()
            cross(side, way, n).start()

    def cross_wait(side, n):
        for way in range(2):
            cross_in(side, way, n).wait_recv()

    local = [
        pltpu.make_async_copy(env_in[0], got.at[0, sec], loc_sem.at[0]),
        pltpu.make_async_copy(env_in[1], got.at[1, sec], loc_sem.at[1]),
        pltpu.make_async_copy(site_in[0], site.at[0], loc_sem.at[2]),
        pltpu.make_async_copy(site_in[1], site.at[1], loc_sem.at[3]),
    ]
    gather_start(0)
    for c in local:
        c.start()

    spread = (lax.broadcasted_iota(jnp.int32, (WR, W), 0) >> 3 == lax.broadcasted_iota(jnp.int32, (WR, W), 1))
    spread = spread.astype(F32).astype(BF)
    spread_t = (lax.broadcasted_iota(jnp.int32, (W, WR), 1) >> 3 == lax.broadcasted_iota(jnp.int32, (W, WR), 0))
    spread_t = spread_t.astype(F32).astype(BF)
    same_row = (
        lax.broadcasted_iota(jnp.int32, (WR, WR), 0) & 7 == lax.broadcasted_iota(jnp.int32, (WR, WR), 1) & 7
    )

    def build_kron(side):
        def body(p, carry):
            op = (table[p].astype(F32) * pattern[p].astype(F32)).astype(BF)
            dims = (((1,), (1,)), ((), ())) if side == 0 else (((1,), (0,)), ((), ()))
            tall = lax.dot_general(spread, op, dims, preferred_element_type=F32).astype(BF)
            full = jnp.where(same_row, dot(tall, spread_t), 0.0).astype(BF)
            kron[side, p] = full
            return carry

        lax.fori_loop(0, CHANNELS, body, 0)

    def build_rows(side):
        pair_row = pl.multiple_of(env // 2 * 16, 16)
        upper = (env % 2).astype(F32)
        for k in range(2):
            live = fan[side][k]
            for g in range(SLOTS // 16):
                block = site[side, pl.ds(k * SLOTS + g * 16, 16), pl.ds(pair_row, 16), :].astype(F32)
                mine = block[:, :R] * (1.0 - upper) + block[:, R:] * upper
                slot = g * 16 + lax.broadcasted_iota(jnp.int32, (16, R, S), 0)
                mine = jnp.where(slot < live, mine, 0.0)
                rows_t[side, k, :, g * 128 : (g + 1) * 128] = mine.reshape(16 * R, S).T.astype(BF)

    def pick(side, q):
        odd = jnp.max((srcv[side][...] == 2 * q + 1).astype(F32), axis=1, keepdims=True)
        return (got[side, q, 0].astype(F32) * (1.0 - odd) + got[side, q, 1].astype(F32) * odd).astype(BF)

    def mix_chip(side, chip):
        rhs = jnp.concatenate([pick(side, chip * 2), pick(side, chip * 2 + 1)], axis=1)

        def body(p, carry):
            r = dot(kron[side, p], rhs).astype(BF)
            mixenv[chip * 2 * CHANNELS + p] = r[:, :S]
            mixenv[(chip * 2 + 1) * CHANNELS + p] = r[:, S:]
            return carry

        lax.fori_loop(0, CHANNELS, body, 0)

    zero = jnp.zeros((S, S), BF)

    def multiply(side, k, lo, hi):
        def body(pair, carry):
            j = k * SLOTS + 2 * pair
            i0 = (src[side][j] >> 1) * CHANNELS + chn[side][j]
            i1 = (src[side][j + 1] >> 1) * CHANNELS + chn[side][j + 1]
            lhs = jnp.concatenate([mixenv[i0], mixenv[i1]], axis=1)
            rhs = jnp.concatenate(
                [
                    jnp.concatenate([site[side, j], zero], axis=1),
                    jnp.concatenate([zero, site[side, j + 1]], axis=1),
                ],
                axis=0,
            )
            r = dot(lhs, rhs)
            both = jnp.concatenate([r[:, :S].reshape(W, R, S), r[:, S:].reshape(W, R, S)], axis=1)
            mixed[:, pl.ds(pl.multiple_of(pair * 16, 16), 16), :] = both.astype(BF)
            return carry

        lax.fori_loop(lo, hi, body, 0)

    def contract(side, k, half):
        u = side * 2 + k

        def body(i, carry):
            v = half * (W // 2) + 2 * i
            r = dot(rows_t[side, k], jnp.concatenate([mixed[v], mixed[v + 1]], axis=1))
            rows = pl.ds(pl.multiple_of(i * 16, 16), 16)
            for e in range(NX * NY):
                t = r[e * R : (e + 1) * R]
                t = jnp.concatenate([t[:, :S], t[:, S:]], axis=0).astype(BF)
                a, b = (e % NX, e // NX) if half == 0 else (e // NX, e % NX)
                send1[u, half, a, b, rows, :] = t
            return carry

        lax.fori_loop(0, W // 4, body, 0)

    def first_copy(u, half, d):
        mine = x if half == 0 else y
        peer = x_peer[d] if half == 0 else y_peer[d]
        return remote(
            send1.at[u, half, lax.rem(mine + d + 1, 4)], recv1.at[u, half, d],
            s1_s.at[u, half, d], s1_r.at[u, half, d], peer,
        )

    def second_copy(u, half, d):
        mine = y if half == 0 else x
        peer = y_peer[d] if half == 0 else x_peer[d]
        return remote(
            send2.at[u, half, lax.rem(mine + d + 1, 4)], recv2.at[u, half, d],
            s2_s.at[u, half, d], s2_r.at[u, half, d], peer,
        )

    def send_first(u, half):
        for d in range(3):
            first_copy(u, half, d).start()

    def sum_first(u):
        for half in range(2):
            mine = x if half == 0 else y
            for d in range(3):
                first_copy(u, half, d).wait_recv()

            def body(b, carry, half=half, mine=mine):
                t = send1[u, half, mine, b].astype(F32)
                for d in range(3):
                    t = t + recv1[u, half, d, b].astype(F32)
                send2[u, half, b] = t.astype(BF)
                return carry

            lax.fori_loop(0, 4, body, 0)
            for d in range(3):
                second_copy(u, half, d).start()

    def sum_second(u):
        for half in range(2):
            mine = y if half == 0 else x
            t = send2[u, half, mine].astype(F32)
            for d in range(3):
                second_copy(u, half, d).wait_recv()
                t = t + recv2[u, half, d].astype(F32)
            out[u // 2][u % 2, half * HALF : (half + 1) * HALF, :] = t.astype(BF)

    build_kron(0)
    build_kron(1)
    local[0].wait()
    cross_in(0, 2, 0).wait_recv()
    cross_in(0, 2, 1).wait_recv()
    mix_chip(0, z)
    for n in range(LAST + 1):
        gather_step(0, n)
        if n == 0:
            local[2].wait()
            build_rows(0)
        if n == 2:
            local[3].wait()
            build_rows(1)
        if n == LAST - 1:
            gather_start(1)
        if n % 2 == 1:
            cross_wait(0, n - 1)
            cross_wait(0, n)
            mix_chip(0, lax.rem(z + NZ - n // 2 - 1, NZ))
            mix_chip(0, lax.rem(z + n // 2 + 1, NZ))
    cross_wait(0, LAST)
    mix_chip(0, lax.rem(z + NZ // 2, NZ))

    for seg in range(4):
        multiply(0, 0, seg * 8, seg * 8 + 8)
        gather_step(1, seg)
    contract(0, 0, 0)
    send_first(0, 0)
    contract(0, 0, 1)
    send_first(0, 1)
    for seg in range(4):
        multiply(0, 1, seg * 8, seg * 8 + 8)
        if seg < 3:
            gather_step(1, seg + 4)
    contract(0, 1, 0)
    send_first(1, 0)
    contract(0, 1, 1)
    send_first(1, 1)

    local[1].wait()
    for n in range(2):
        cross_in(1, 2, n).wait_recv()
    for n in range(LAST + 1):
        cross_wait(1, n)
    sum_first(0)

    def mix_right(lo, hi):
        def body(chip, carry):
            mix_chip(1, chip)
            return carry

        lax.fori_loop(lo, hi, body, 0)

    mix_right(0, NZ // 2)
    sum_first(1)
    mix_right(NZ // 2, NZ)
    for k in range(2):
        multiply(1, k, 0, 32)
        for half in range(2):
            contract(1, k, half)
            send_first(2 + k, half)
        sum_second(k)
    for u in (2, 3):
        sum_first(u)
    for u in (2, 3):
        sum_second(u)

    for side in range(2):
        for n in range(LAST + 1):
            for way in range(2):
                ring(side, way, n).wait_send()
                cross(side, way, n).wait_send()
        for n in range(2):
            cross(side, 2, n).wait_send()
    for u in range(4):
        for half in range(2):
            for d in range(3):
                first_copy(u, half, d).wait_send()
                second_copy(u, half, d).wait_send()


def per_device(
    env_left, env_right, site_left, site_right, source_left, source_right, channel_left, channel_right,
    fanin_left, fanin_right, operator_table, operator_pattern,
):
    smem = pl.BlockSpec(memory_space=pltpu.SMEM)
    vmem = pl.BlockSpec(memory_space=pltpu.VMEM)
    hbm = pl.BlockSpec(memory_space=pl.ANY)
    dma = pltpu.SemaphoreType.DMA
    new_left, new_right = pl.pallas_call(
        kernel,
        out_shape=[jax.ShapeDtypeStruct((2, WR, S), BF)] * 2,
        in_specs=[smem] * 6 + [vmem] * 4 + [hbm] * 4,
        out_specs=[vmem, vmem],
        scratch_shapes=[
            pltpu.VMEM((2, 2 * NZ, 2, WR, S), BF),
            pltpu.VMEM((2, 2 * SLOTS, S, S), BF),
            pltpu.VMEM((2, CHANNELS, WR, WR), BF),
            pltpu.VMEM((2 * NZ * CHANNELS, WR, S), BF),
            pltpu.VMEM((W, SLOTS * R, S), BF),
            pltpu.VMEM((2, 2, S, SLOTS * R), BF),
            pltpu.VMEM((4, 2, 4, 4, HALF, S), BF),
            pltpu.VMEM((4, 2, 3, 4, HALF, S), BF),
            pltpu.VMEM((4, 2, 4, HALF, S), BF),
            pltpu.VMEM((4, 2, 3, HALF, S), BF),
            dma((4,)),
            dma((2, 2, LAST + 1)),
            dma((2, 2, LAST + 1)),
            dma((2, 2 * NZ)),
            dma((2, 2 * NZ)),
            dma((4, 2, 3)),
            dma((4, 2, 3)),
            dma((4, 2, 3)),
            dma((4, 2, 3)),
        ],
        compiler_params=pltpu.CompilerParams(
            collective_id=0, has_side_effects=True, vmem_limit_bytes=60 * 2**20
        ),
    )(
        fanin_left, fanin_right, source_left, source_right, channel_left, channel_right,
        source_left.reshape(1, -1), source_right.reshape(1, -1), operator_table, operator_pattern,
        env_left.reshape(2, WR, S), env_right.reshape(2, WR, S), site_left, site_right,
    )
    return new_left.reshape(2, W, R, S), new_right.reshape(2, W, R, S)


def solution(mesh):
    wide, flat = P("sec", None, "env", None), P("sec")
    return jax.shard_map(
        per_device,
        mesh=mesh,
        in_specs=(wide, wide, P("sec", None, None), P("sec", None, None)) + (flat,) * 6 + (P(), P()),
        out_specs=(wide, wide),
        check_vma=False,
    )
```

time: 315 us -> 121 us (0.38)
  waiting for transfers between devices: 152 us -> 0 us
  Pallas kernels: 0 us -> 117 us
  local copies, waits for them, and re-layouts: 82.6 us -> 3.19 us
  matrix products: 53.8 us -> 0 us
  between operations: 14.6 us -> 0.64 us
  other arithmetic: 10.8 us -> 0 us
    unnamed x4 -> x0, waiting for transfers between devices: 122 us -> none
    pallas_call x0 -> x1, Pallas kernels: none -> 117 us  [per_device(): pl.pallas_call(kernel, out_shape=[jax.ShapeDtypeStruct((2, WR, S), BF)] *...]
    dot_general x8 -> x0, matrix products: 53.8 us -> none  [the longest x2 21.4 us: contract(): lax.dot_general(mix_flat, first_section, (((1,), (1,)), ((0,), (0,))), pr...]
    reshape x4 -> x0, local copies, waits for them, and re-layouts: 33 us -> none  [the longest x2 32.7 us: contract(): first_section = first_section.reshape(batch, channels, row_count * states)]
    all_gather x2 -> x0, waiting for transfers between devices: 29.8 us -> none  [fetch_tiles(): everything = lax.all_gather(old_tiles, 'sec', axis=0, tiled=True)]
    unnamed x12 -> x2, local copies, waits for them, and re-layouts: 23.7 us -> 3.19 us
    gather x2 -> x0, local copies, waits for them, and re-layouts: 18.6 us -> none  [fetch_tiles(): return jnp.take(everything, source, axis=0)]
    select_n x4 -> x0, other arithmetic: 8.31 us -> none  [the longest x2 7 us: rebuild(): jnp.where(live_slots[:, None, None], site_blocks, jnp.zeros_like(site_blo...]
  transfers between devices with their start and end apart: 3 -> 0, of which waited for: 2 -> 0; matrix products, arithmetic and copies ran while one was open for 26% -> 0% of each run, Pallas kernels for 0% -> 0%
where the time goes in v1:
time: 121 us
  Pallas kernels  117 us (97%)
  local copies, waits for them, and re-layouts  3.19 us (3%)
    pallas_call x1, Pallas kernels, per_device(): pl.pallas_call(kernel, out_shape=[jax.ShapeDtypeStruct((2, WR, S), BF)] *...  117 us
    unnamed x2, local copies, waits for them, and re-layouts  3.19 us

profile of v1, /device:TPU:1, one launch (start us, length us, event | category | flops | bytes accessed | tf_op | source)
XLA Modules:
  0.0 120.9 jit_solution(9914642519201819014)
XLA Ops:
  0.6 117.1 %shard_map.131 = (bf16[2,320,128]{2,1,0:T(8,128)(2,1)}, bf16[2,320,128]{2,1,0:T(8,128)(2,1)}) custom-call(s32[2]{0:T(128)} %fan_l.1, s32[2]{0:T(128)} %fan_r.1, s32[128]{0:T(128)} %src_l.1, s32[128]{0:T(128)} %src_r.1, s32[128]{0:T(128)} %chn_l.1, s32[128]{0:T(128)} %chn_r.1, s32[1,128]{1,0:T(1,128)} %bitcast.10, s32[1,128]{1,0:T(1,128)} %bitcast.11, ...), custom_call_target="tpu_custom_call" | custom-call | tf_op jit(solution)/shard_map/pallas_call | solution.py:336
  117.7 1.6 %copy.16 = bf16[2,40,8,128]{3,2,1,0:T(8,128)(2,1)} copy(bf16[2,40,8,128]{3,2,1,0:T(8,128)(2,1)} %bitcast.7) | data formatting | bytes 327680
  119.3 1.6 %copy.17 = bf16[2,40,8,128]{3,2,1,0:T(8,128)(2,1)} copy(bf16[2,40,8,128]{3,2,1,0:T(8,128)(2,1)} %bitcast.6) | data formatting | bytes 327680

commit v2 on v1

--- a/solution.py
+++ b/solution.py
@@ -157,29 +157,24 @@
             mixenv[(chip * 2 + 1) * CHANNELS + p] = r[:, S:]
             return carry
 
-        lax.fori_loop(0, CHANNELS, body, 0)
-
-    zero = jnp.zeros((S, S), BF)
-
-    def multiply(side, k, lo, hi):
-        def body(pair, carry):
-            j = k * SLOTS + 2 * pair
-            i0 = (src[side][j] >> 1) * CHANNELS + chn[side][j]
-            i1 = (src[side][j + 1] >> 1) * CHANNELS + chn[side][j + 1]
-            lhs = jnp.concatenate([mixenv[i0], mixenv[i1]], axis=1)
-            rhs = jnp.concatenate(
-                [
-                    jnp.concatenate([site[side, j], zero], axis=1),
-                    jnp.concatenate([zero, site[side, j + 1]], axis=1),
-                ],
-                axis=0,
-            )
-            r = dot(lhs, rhs)
-            both = jnp.concatenate([r[:, :S].reshape(W, R, S), r[:, S:].reshape(W, R, S)], axis=1)
-            mixed[:, pl.ds(pl.multiple_of(pair * 16, 16), 16), :] = both.astype(BF)
-            return carry
-
-        lax.fori_loop(lo, hi, body, 0)
+        lax.fori_loop(0, CHANNELS, body, 0, unroll=True)
+
+    def multiply(side, k, hooks=()):
+        def part(seg, carry):
+            for i in range(8):
+                pair = seg * 8 + i
+                j = k * SLOTS + 2 * pair
+                i0 = (src[side][j] >> 1) * CHANNELS + chn[side][j]
+                i1 = (src[side][j + 1] >> 1) * CHANNELS + chn[side][j + 1]
+                r0 = dot(mixenv[i0], site[side, j]).reshape(W, R, S)
+                r1 = dot(mixenv[i1], site[side, j + 1]).reshape(W, R, S)
+                both = jnp.concatenate([r0, r1], axis=1).astype(BF)
+                mixed[:, pl.ds(pl.multiple_of(pair * 16, 16), 16), :] = both
+            for i, hook in enumerate(hooks):
+                pl.when(seg == i)(hook)
+            return carry
+
+        lax.fori_loop(0, SLOTS // 16, part, 0)
 
     def contract(side, k, half):
         u = side * 2 + k
@@ -195,7 +190,7 @@
                 send1[u, half, a, b, rows, :] = t
             return carry
 
-        lax.fori_loop(0, W // 4, body, 0)
+        lax.fori_loop(0, W // 4, body, 0, unroll=True)
 
     def first_copy(u, half, d):
         mine = x if half == 0 else y
@@ -267,21 +262,14 @@
     cross_wait(0, LAST)
     mix_chip(0, lax.rem(z + NZ // 2, NZ))
 
-    for seg in range(4):
-        multiply(0, 0, seg * 8, seg * 8 + 8)
-        gather_step(1, seg)
-    contract(0, 0, 0)
-    send_first(0, 0)
-    contract(0, 0, 1)
-    send_first(0, 1)
-    for seg in range(4):
-        multiply(0, 1, seg * 8, seg * 8 + 8)
-        if seg < 3:
-            gather_step(1, seg + 4)
-    contract(0, 1, 0)
-    send_first(1, 0)
-    contract(0, 1, 1)
-    send_first(1, 1)
+    multiply(0, 0, [functools.partial(gather_step, 1, n) for n in range(4)])
+    for half in range(2):
+        contract(0, 0, half)
+        send_first(0, half)
+    multiply(0, 1, [functools.partial(gather_step, 1, n) for n in range(4, 7)])
+    for half in range(2):
+        contract(0, 1, half)
+        send_first(1, half)
 
     local[1].wait()
     for n in range(2):
@@ -301,7 +289,7 @@
     sum_first(1)
     mix_right(NZ // 2, NZ)
     for k in range(2):
-        multiply(1, k, 0, 32)
+        multiply(1, k)
         for half in range(2):
             contract(1, k, half)
             send_first(2 + k, half)

time: 121 us -> 92 us (0.76); the launches traced: 121 us -> 90.5 us
  Pallas kernels: 117 us -> 86.7 us
    pallas_call x1, Pallas kernels: 117 us -> 86.7 us  [per_device(): pl.pallas_call(kernel, out_shape=[jax.ShapeDtypeStruct((2, WR, S), BF)] *...]
where the time goes in v2:
time: 92 us; the launch traced here: 90.5 us
  Pallas kernels  86.7 us (94%)
  local copies, waits for them, and re-layouts  3.19 us (3%)
    pallas_call x1, Pallas kernels, per_device(): pl.pallas_call(kernel, out_shape=[jax.ShapeDtypeStruct((2, WR, S), BF)] *...  86.7 us
    unnamed x2, local copies, waits for them, and re-layouts  3.19 us

profile of v2, /device:TPU:1, one launch (start us, length us, event | category | flops | bytes accessed | tf_op | source)
XLA Modules:
  0.0 90.5 jit_solution(16554457608715746298)
XLA Ops:
  0.6 86.7 %shard_map.131 = (bf16[2,320,128]{2,1,0:T(8,128)(2,1)}, bf16[2,320,128]{2,1,0:T(8,128)(2,1)}) custom-call(s32[2]{0:T(128)} %fan_l.1, s32[2]{0:T(128)} %fan_r.1, s32[128]{0:T(128)} %src_l.1, s32[128]{0:T(128)} %src_r.1, s32[128]{0:T(128)} %chn_l.1, s32[128]{0:T(128)} %chn_r.1, s32[1,128]{1,0:T(1,128)} %bitcast.10, s32[1,128]{1,0:T(1,128)} %bitcast.11, ...), custom_call_target="tpu_custom_call" | custom-call | tf_op jit(solution)/shard_map/pallas_call | solution.py:324
  87.3 1.6 %copy.16 = bf16[2,40,8,128]{3,2,1,0:T(8,128)(2,1)} copy(bf16[2,40,8,128]{3,2,1,0:T(8,128)(2,1)} %bitcast.7) | data formatting | bytes 327680
  88.9 1.6 %copy.17 = bf16[2,40,8,128]{3,2,1,0:T(8,128)(2,1)} copy(bf16[2,40,8,128]{3,2,1,0:T(8,128)(2,1)} %bitcast.6) | data formatting | bytes 327680

commit v3 on v2

--- a/solution.py
+++ b/solution.py
@@ -25,7 +25,7 @@
     fan_l, fan_r, src_l, src_r, chn_l, chn_r, srcv_l, srcv_r, table, pattern, env_l, env_r, site_l, site_r,
     out_l, out_r,
     got, site, kron, mixenv, mixed, rows_t, send1, recv1, send2, recv2,
-    loc_sem, ring_s, ring_r, cross_s, cross_r, s1_s, s1_r, s2_s, s2_r,
+    slot_at, source_of, loc_sem, ring_s, ring_r, cross_s, cross_r, s1_s, s1_r, s2_s, s2_r,
 ):
     fan, src, chn, srcv = (fan_l, fan_r), (src_l, src_r), (chn_l, chn_r), (srcv_l, srcv_r)
     env_in, site_in, out = (env_l, env_r), (site_l, site_r), (out_l, out_r)
@@ -121,7 +121,7 @@
         lax.broadcasted_iota(jnp.int32, (WR, WR), 0) & 7 == lax.broadcasted_iota(jnp.int32, (WR, WR), 1) & 7
     )
 
-    def build_kron(side):
+    def build_kron(side, lo, hi):
         def body(p, carry):
             op = (table[p].astype(F32) * pattern[p].astype(F32)).astype(BF)
             dims = (((1,), (1,)), ((), ())) if side == 0 else (((1,), (0,)), ((), ()))
@@ -130,22 +130,27 @@
             kron[side, p] = full
             return carry
 
-        lax.fori_loop(0, CHANNELS, body, 0)
+        lax.fori_loop(lo, hi, body, 0, unroll=4)
 
     def build_rows(side):
         pair_row = pl.multiple_of(env // 2 * 16, 16)
         upper = (env % 2).astype(F32)
+
         for k in range(2):
             live = fan[side][k]
-            for g in range(SLOTS // 16):
+
+            def body(g, carry, k=k, live=live):
                 block = site[side, pl.ds(k * SLOTS + g * 16, 16), pl.ds(pair_row, 16), :].astype(F32)
                 mine = block[:, :R] * (1.0 - upper) + block[:, R:] * upper
                 slot = g * 16 + lax.broadcasted_iota(jnp.int32, (16, R, S), 0)
                 mine = jnp.where(slot < live, mine, 0.0)
-                rows_t[side, k, :, g * 128 : (g + 1) * 128] = mine.reshape(16 * R, S).T.astype(BF)
+                rows_t[side, k, g] = mine.reshape(16 * R, S).T.astype(BF)
+                return carry
+
+            lax.fori_loop(0, SLOTS // 16, body, 0)
 
     def pick(side, q):
-        odd = jnp.max((srcv[side][...] == 2 * q + 1).astype(F32), axis=1, keepdims=True)
+        odd = jnp.max((source_of[side] == 2 * q + 1).astype(F32), axis=1, keepdims=True)
         return (got[side, q, 0].astype(F32) * (1.0 - odd) + got[side, q, 1].astype(F32) * odd).astype(BF)
 
     def mix_chip(side, chip):
@@ -159,75 +164,85 @@
 
         lax.fori_loop(0, CHANNELS, body, 0, unroll=True)
 
-    def multiply(side, k, hooks=()):
+    def multiply(side, k, hook):
         def part(seg, carry):
             for i in range(8):
                 pair = seg * 8 + i
                 j = k * SLOTS + 2 * pair
-                i0 = (src[side][j] >> 1) * CHANNELS + chn[side][j]
-                i1 = (src[side][j + 1] >> 1) * CHANNELS + chn[side][j + 1]
-                r0 = dot(mixenv[i0], site[side, j]).reshape(W, R, S)
-                r1 = dot(mixenv[i1], site[side, j + 1]).reshape(W, R, S)
+                r0 = dot(mixenv[slot_at[side, j]], site[side, j]).reshape(W, R, S)
+                r1 = dot(mixenv[slot_at[side, j + 1]], site[side, j + 1]).reshape(W, R, S)
                 both = jnp.concatenate([r0, r1], axis=1).astype(BF)
                 mixed[:, pl.ds(pl.multiple_of(pair * 16, 16), 16), :] = both
-            for i, hook in enumerate(hooks):
-                pl.when(seg == i)(hook)
+            hook(seg)
             return carry
 
         lax.fori_loop(0, SLOTS // 16, part, 0)
 
     def contract(side, k, half):
         u = side * 2 + k
-
-        def body(i, carry):
+        left = jnp.concatenate([rows_t[side, k, g] for g in range(SLOTS // 16)], axis=1)
+        for i in range(W // 4):
             v = half * (W // 2) + 2 * i
-            r = dot(rows_t[side, k], jnp.concatenate([mixed[v], mixed[v + 1]], axis=1))
-            rows = pl.ds(pl.multiple_of(i * 16, 16), 16)
+            r = dot(left, jnp.concatenate([mixed[v], mixed[v + 1]], axis=1))
             for e in range(NX * NY):
                 t = r[e * R : (e + 1) * R]
                 t = jnp.concatenate([t[:, :S], t[:, S:]], axis=0).astype(BF)
-                a, b = (e % NX, e // NX) if half == 0 else (e // NX, e % NX)
-                send1[u, half, a, b, rows, :] = t
-            return carry
-
-        lax.fori_loop(0, W // 4, body, 0, unroll=True)
-
-    def first_copy(u, half, d):
-        mine = x if half == 0 else y
-        peer = x_peer[d] if half == 0 else y_peer[d]
+                a = (1 - half) * (e % NX) + half * (e // NX)
+                b = (1 - half) * (e // NX) + half * (e % NX)
+                send1[u, half, a, b, i * 16 : (i + 1) * 16, :] = t
+
+    def along(half, d):
+        on_x, on_y = lax.rem(x + d + 1, NX), lax.rem(y + d + 1, NY)
+        to_x, to_y = y * NX + on_x, on_y * NX + x
+        first = (1 - half) * on_x + half * on_y, (sec, (1 - half) * to_x + half * to_y)
+        second = (1 - half) * on_y + half * on_x, (sec, (1 - half) * to_y + half * to_x)
+        return first, second
+
+    def first_copy(u, half, c):
+        ahead = c in (0, 2, 4)
+        spot = along(half, 1)[0][0] if c < 2 else along(half, 0 if ahead else 2)[0][0]
+        part = pl.ds(0 if c in (0, 3, 4) else 2, 2)
         return remote(
-            send1.at[u, half, lax.rem(mine + d + 1, 4)], recv1.at[u, half, d],
-            s1_s.at[u, half, d], s1_r.at[u, half, d], peer,
+            send1.at[u, half, spot, part], recv1.at[u, half, c],
+            s1_s.at[u, half, c], s1_r.at[u, half, c], along(half, 0 if ahead else 2)[0][1],
         )
 
     def second_copy(u, half, d):
-        mine = y if half == 0 else x
-        peer = y_peer[d] if half == 0 else x_peer[d]
-        return remote(
-            send2.at[u, half, lax.rem(mine + d + 1, 4)], recv2.at[u, half, d],
-            s2_s.at[u, half, d], s2_r.at[u, half, d], peer,
-        )
+        spot, peer = along(half, d)[1]
+        return remote(send2.at[u, half, spot], recv2.at[u, half, d], s2_s.at[u, half, d], s2_r.at[u, half, d], peer)
 
     def send_first(u, half):
-        for d in range(3):
-            first_copy(u, half, d).start()
+        for c in range(4):
+            first_copy(u, half, c).start()
+
+    def pass_on(u):
+        def body(half, carry):
+            for c in range(2):
+                first_copy(u, half, c).wait_recv()
+                spot = along(half, 2 * c)[0][0]
+                for b in range(2):
+                    t = send1[u, half, spot, 2 * c + b].astype(F32) + recv1[u, half, c, b].astype(F32)
+                    send1[u, half, spot, 2 * c + b] = t.astype(BF)
+                first_copy(u, half, 4 + c).start()
+            return carry
+
+        lax.fori_loop(0, 2, body, 0)
 
     def sum_first(u):
-        for half in range(2):
-            mine = x if half == 0 else y
-            for d in range(3):
-                first_copy(u, half, d).wait_recv()
-
-            def body(b, carry, half=half, mine=mine):
+        def body(half, carry):
+            mine = (1 - half) * x + half * y
+            for c in range(2, 6):
+                first_copy(u, half, c).wait_recv()
+            for b in range(4):
+                one, two = (3, 4) if b < 2 else (2, 5)
                 t = send1[u, half, mine, b].astype(F32)
-                for d in range(3):
-                    t = t + recv1[u, half, d, b].astype(F32)
+                t = t + recv1[u, half, one, b % 2].astype(F32) + recv1[u, half, two, b % 2].astype(F32)
                 send2[u, half, b] = t.astype(BF)
-                return carry
-
-            lax.fori_loop(0, 4, body, 0)
             for d in range(3):
                 second_copy(u, half, d).start()
+            return carry
+
+        lax.fori_loop(0, 2, body, 0)
 
     def sum_second(u):
         for half in range(2):
@@ -238,66 +253,150 @@
                 t = t + recv2[u, half, d].astype(F32)
             out[u // 2][u % 2, half * HALF : (half + 1) * HALF, :] = t.astype(BF)
 
-    build_kron(0)
-    build_kron(1)
+    for side in range(2):
+        source_of[side] = srcv[side][...]
+
+        def place(j, carry, side=side):
+            slot_at[side, j] = (src[side][j] >> 1) * CHANNELS + chn[side][j]
+            return carry
+
+        lax.fori_loop(0, 2 * SLOTS, place, 0, unroll=8)
+    build_kron(0, 0, CHANNELS)
     local[0].wait()
-    cross_in(0, 2, 0).wait_recv()
-    cross_in(0, 2, 1).wait_recv()
-    mix_chip(0, z)
-    for n in range(LAST + 1):
-        gather_step(0, n)
-        if n == 0:
+
+    def before_mix(side, i):
+        def at(which, step):
+            return pl.when((side == which) & (i == step))
+
+        @at(0, 0)
+        def _():
+            gather_step(0, 0)
+
+        @at(0, 1)
+        def _():
+            gather_step(0, 1)
+
+        @at(0, 3)
+        def _():
+            gather_step(0, 2)
             local[2].wait()
             build_rows(0)
-        if n == 2:
-            local[3].wait()
-            build_rows(1)
-        if n == LAST - 1:
+            gather_step(0, 3)
+
+        @at(0, 5)
+        def _():
+            gather_step(0, 4)
+            build_kron(1, 0, CHANNELS)
+            gather_step(0, 5)
             gather_start(1)
-        if n % 2 == 1:
-            cross_wait(0, n - 1)
-            cross_wait(0, n)
-            mix_chip(0, lax.rem(z + NZ - n // 2 - 1, NZ))
-            mix_chip(0, lax.rem(z + n // 2 + 1, NZ))
-    cross_wait(0, LAST)
-    mix_chip(0, lax.rem(z + NZ // 2, NZ))
-
-    multiply(0, 0, [functools.partial(gather_step, 1, n) for n in range(4)])
-    for half in range(2):
-        contract(0, 0, half)
-        send_first(0, half)
-    multiply(0, 1, [functools.partial(gather_step, 1, n) for n in range(4, 7)])
-    for half in range(2):
-        contract(0, 1, half)
-        send_first(1, half)
-
-    local[1].wait()
-    for n in range(2):
-        cross_in(1, 2, n).wait_recv()
-    for n in range(LAST + 1):
-        cross_wait(1, n)
-    sum_first(0)
-
-    def mix_right(lo, hi):
-        def body(chip, carry):
-            mix_chip(1, chip)
-            return carry
-
-        lax.fori_loop(lo, hi, body, 0)
-
-    mix_right(0, NZ // 2)
-    sum_first(1)
-    mix_right(NZ // 2, NZ)
-    for k in range(2):
-        multiply(1, k)
-        for half in range(2):
-            contract(1, k, half)
-            send_first(2 + k, half)
-        sum_second(k)
-    for u in (2, 3):
-        sum_first(u)
-    for u in (2, 3):
-        sum_second(u)
+
+        @at(0, 7)
+        def _():
+            gather_step(0, 6)
+
+        @at(1, 0)
+        def _():
+            local[1].wait()
+
+        @at(1, 1)
+        def _():
+            gather_step(1, 4)
+
+        @at(1, 2)
+        def _():
+            pass_on(1)
+
+        @at(1, 3)
+        def _():
+            gather_step(1, 5)
+
+        @at(1, 4)
+        def _():
+            sum_first(0)
+
+        @at(1, 5)
+        def _():
+            gather_step(1, 6)
+
+        @at(1, 7)
+        def _():
+            sum_first(1)
+
+        @pl.when(i == 0)
+        def _():
+            cross_in(side, 2, 0).wait_recv()
+            cross_in(side, 2, 1).wait_recv()
+
+        for n in range(0, LAST, 2):
+
+            @pl.when(i == n + 1)
+            def _(n=n):
+                cross_wait(side, n)
+                cross_wait(side, n + 1)
+
+        @pl.when(i == LAST + 1)
+        def _():
+            cross_wait(side, LAST)
+
+    def one_side(side, carry):
+        def mix_one(i, carry):
+            before_mix(side, i)
+            far = (i + 1) // 2
+            mix_chip(side, lax.rem(z + NZ + far * (1 - 2 * (i % 2)), NZ))
+            return carry
+
+        lax.fori_loop(0, NZ, mix_one, 0)
+
+        def one_sector(k, carry):
+            def during(seg):
+                @pl.when((side == 0) & (k == 0) & (seg == 3))
+                def _():
+                    gather_step(1, 0)
+
+                @pl.when((side == 0) & (k == 1) & (seg == 0))
+                def _():
+                    gather_step(1, 1)
+
+                @pl.when((side == 0) & (k == 1) & (seg == 2))
+                def _():
+                    gather_step(1, 2)
+
+                @pl.when((side == 1) & (k == 1) & (seg == 3))
+                def _():
+                    pass_on(2)
+
+            multiply(side, k, during)
+
+            def one_half(half, carry):
+                contract(side, k, half)
+                send_first(side * 2 + k, half)
+                return carry
+
+            lax.fori_loop(0, 2, one_half, 0)
+
+            @pl.when((side == 0) & (k == 1))
+            def _():
+                pass_on(0)
+                gather_step(1, 3)
+                local[3].wait()
+                build_rows(1)
+
+            @pl.when((side == 1) & (k == 0))
+            def _():
+                sum_second(0)
+
+            return carry
+
+        lax.fori_loop(0, 2, one_sector, 0)
+        return carry
+
+    lax.fori_loop(0, 2, one_side, 0)
+    pass_on(3)
+    sum_second(1)
+    sum_first(2)
+    sum_first(3)
+    sum_second(2)
+    sum_second(3)
 
     for side in range(2):
         for n in range(LAST + 1):
@@ -308,8 +407,9 @@
             cross(side, 2, n).wait_send()
     for u in range(4):
         for half in range(2):
+            for c in range(6):
+                first_copy(u, half, c).wait_send()
             for d in range(3):
-                first_copy(u, half, d).wait_send()
                 second_copy(u, half, d).wait_send()
 
 
@@ -332,18 +432,20 @@
             pltpu.VMEM((2, CHANNELS, WR, WR), BF),
             pltpu.VMEM((2 * NZ * CHANNELS, WR, S), BF),
             pltpu.VMEM((W, SLOTS * R, S), BF),
-            pltpu.VMEM((2, 2, S, SLOTS * R), BF),
+            pltpu.VMEM((2, 2, SLOTS // 16, S, 16 * R), BF),
             pltpu.VMEM((4, 2, 4, 4, HALF, S), BF),
-            pltpu.VMEM((4, 2, 3, 4, HALF, S), BF),
+            pltpu.VMEM((4, 2, 6, 2, HALF, S), BF),
             pltpu.VMEM((4, 2, 4, HALF, S), BF),
             pltpu.VMEM((4, 2, 3, HALF, S), BF),
+            pltpu.SMEM((2, 2 * SLOTS), jnp.int32),
+            pltpu.VMEM((2, 1, 2 * SLOTS), jnp.int32),
             dma((4,)),
             dma((2, 2, LAST + 1)),
             dma((2, 2, LAST + 1)),
             dma((2, 2 * NZ)),
             dma((2, 2 * NZ)),
-            dma((4, 2, 3)),
-            dma((4, 2, 3)),
+            dma((4, 2, 6)),
+            dma((4, 2, 6)),
             dma((4, 2, 3)),
             dma((4, 2, 3)),
         ],

time: 92 us -> 81.9 us (0.89)
  Pallas kernels: 86.7 us -> 76.5 us
    pallas_call x1, Pallas kernels: 86.7 us -> 76.5 us  [per_device(): pl.pallas_call(kernel, out_shape=[jax.ShapeDtypeStruct((2, WR, S), BF)] *...]
where the time goes in v3:
time: 81.9 us; the launch traced here: 80.3 us
  Pallas kernels  76.5 us (93%)
  local copies, waits for them, and re-layouts  3.19 us (4%)
    pallas_call x1, Pallas kernels, per_device(): pl.pallas_call(kernel, out_shape=[jax.ShapeDtypeStruct((2, WR, S), BF)] *...  76.5 us
    unnamed x2, local copies, waits for them, and re-layouts  3.19 us

profile of v3, /device:TPU:1, one launch (start us, length us, event | category | flops | bytes accessed | tf_op | source)
XLA Modules:
  0.0 80.3 jit_solution(1286835398073201148)
XLA Ops:
  0.6 76.5 %shard_map.131 = (bf16[2,320,128]{2,1,0:T(8,128)(2,1)}, bf16[2,320,128]{2,1,0:T(8,128)(2,1)}) custom-call(s32[2]{0:T(128)} %fan_l.1, s32[2]{0:T(128)} %fan_r.1, s32[128]{0:T(128)} %src_l.1, s32[128]{0:T(128)} %src_r.1, s32[128]{0:T(128)} %chn_l.1, s32[128]{0:T(128)} %chn_r.1, s32[1,128]{1,0:T(1,128)} %bitcast.10, s32[1,128]{1,0:T(1,128)} %bitcast.11, ...), custom_call_target="tpu_custom_call" | custom-call | tf_op jit(solution)/shard_map/pallas_call | solution.py:424
  77.1 1.6 %copy.16 = bf16[2,40,8,128]{3,2,1,0:T(8,128)(2,1)} copy(bf16[2,40,8,128]{3,2,1,0:T(8,128)(2,1)} %bitcast.7) | data formatting | bytes 327680
  78.7 1.6 %copy.17 = bf16[2,40,8,128]{3,2,1,0:T(8,128)(2,1)} copy(bf16[2,40,8,128]{3,2,1,0:T(8,128)(2,1)} %bitcast.6) | data formatting | bytes 327680

commit v4 on v3

--- a/solution.py
+++ b/solution.py
@@ -25,9 +25,9 @@
     fan_l, fan_r, src_l, src_r, chn_l, chn_r, srcv_l, srcv_r, table, pattern, env_l, env_r, site_l, site_r,
     out_l, out_r,
     got, site, kron, mixenv, mixed, rows_t, send1, recv1, send2, recv2,
-    slot_at, source_of, loc_sem, ring_s, ring_r, cross_s, cross_r, s1_s, s1_r, s2_s, s2_r,
+    lists, slot_at, source_of, loc_sem, ring_s, ring_r, cross_s, cross_r, s1_s, s1_r, s2_s, s2_r,
 ):
-    fan, src, chn, srcv = (fan_l, fan_r), (src_l, src_r), (chn_l, chn_r), (srcv_l, srcv_r)
+    fan = (fan_l, fan_r)
     env_in, site_in, out = (env_l, env_r), (site_l, site_r), (out_l, out_r)
     sec, env = lax.axis_index("sec"), lax.axis_index("env")
     z, core = sec // 2, sec % 2
@@ -55,20 +55,22 @@
         h = n % 2 if n < LAST else way
         return chip, h
 
-    def ring(side, way, n):
+    def ring(side, way, n, part):
         peer = up if way == 0 else down
+        rows = pl.ds(part * HALF, HALF)
         if n < 2:
-            a, chip, h = env_in[side].at[n], z, n
+            a, chip, h = env_in[side].at[n, rows], z, n
         else:
             back = n - 2 if (n < LAST or way == 0) else n - 1
             chip, h = chunk_of(way, back)
-            a = got.at[side, chip * 2 + core, h]
-        return remote(a, got.at[side, chip * 2 + core, h], ring_s.at[side, way, n], ring_r.at[side, way, n], peer)
-
-    def ring_in(side, way, n):
+            a = got.at[side, chip * 2 + core, h, rows]
+        b = got.at[side, chip * 2 + core, h, rows]
+        return remote(a, b, ring_s.at[side, way, n, part], ring_r.at[side, way, n, part], peer)
+
+    def ring_in(side, way, n, part):
         chip, h = chunk_of(way, n)
-        spot = got.at[side, chip * 2 + core, h]
-        return remote(spot, spot, ring_s.at[side, way, n], ring_r.at[side, way, n], up if way == 0 else down)
+        spot = got.at[side, chip * 2 + core, h, pl.ds(part * HALF, HALF)]
+        return remote(spot, spot, ring_s.at[side, way, n, part], ring_r.at[side, way, n, part], up if way == 0 else down)
 
     def cross(side, way, n):
         if way == 2:
@@ -85,18 +87,21 @@
 
     def gather_start(side):
         for n in range(2):
-            ring(side, 0, n).start()
-            ring(side, 1, n).start()
+            for part in range(2):
+                ring(side, 0, n, part).start()
+                ring(side, 1, n, part).start()
         for n in range(2):
             cross(side, 2, n).start()
 
     def gather_step(side, n):
+        for part in range(2):
+            for way in range(2):
+                ring_in(side, way, n, part).wait_recv()
+                for later in range(2, LAST + 1):
+                    back = later - 2 if (later < LAST or way == 0) else later - 1
+                    if back == n:
+                        ring(side, way, later, part).start()
         for way in range(2):
-            ring_in(side, way, n).wait_recv()
-            for later in range(2, LAST + 1):
-                back = later - 2 if (later < LAST or way == 0) else later - 1
-                if back == n:
-                    ring(side, way, later).start()
             cross(side, way, n).start()
 
     def cross_wait(side, n):
@@ -109,8 +114,10 @@
         pltpu.make_async_copy(site_in[0], site.at[0], loc_sem.at[2]),
         pltpu.make_async_copy(site_in[1], site.at[1], loc_sem.at[3]),
     ]
+    small = [pltpu.make_async_copy(a, lists.at[i], loc_sem.at[4 + i]) for i, a in enumerate((src_l, src_r, chn_l, chn_r))]
+    small += [pltpu.make_async_copy(a, source_of.at[i], loc_sem.at[8 + i]) for i, a in enumerate((srcv_l, srcv_r))]
     gather_start(0)
-    for c in local:
+    for c in small + local:
         c.start()
 
     spread = (lax.broadcasted_iota(jnp.int32, (WR, W), 0) >> 3 == lax.broadcasted_iota(jnp.int32, (WR, W), 1))
@@ -150,8 +157,8 @@
             lax.fori_loop(0, SLOTS // 16, body, 0)
 
     def pick(side, q):
-        odd = jnp.max((source_of[side] == 2 * q + 1).astype(F32), axis=1, keepdims=True)
-        return (got[side, q, 0].astype(F32) * (1.0 - odd) + got[side, q, 1].astype(F32) * odd).astype(BF)
+        odd = jnp.max((source_of[side] == 2 * q + 1).astype(F32), axis=1, keepdims=True).astype(BF)
+        return got[side, q, 0] * (1 - odd) + got[side, q, 1] * odd
 
     def mix_chip(side, chip):
         rhs = jnp.concatenate([pick(side, chip * 2), pick(side, chip * 2 + 1)], axis=1)
@@ -166,8 +173,8 @@
 
     def multiply(side, k, hook):
         def part(seg, carry):
-            for i in range(8):
-                pair = seg * 8 + i
+            for i in range(16):
+                pair = seg * 16 + i
                 j = k * SLOTS + 2 * pair
                 r0 = dot(mixenv[slot_at[side, j]], site[side, j]).reshape(W, R, S)
                 r1 = dot(mixenv[slot_at[side, j + 1]], site[side, j + 1]).reshape(W, R, S)
@@ -176,7 +183,7 @@
             hook(seg)
             return carry
 
-        lax.fori_loop(0, SLOTS // 16, part, 0)
+        lax.fori_loop(0, SLOTS // 32, part, 0)
 
     def contract(side, k, half):
         u = side * 2 + k
@@ -253,15 +260,16 @@
                 t = t + recv2[u, half, d].astype(F32)
             out[u // 2][u % 2, half * HALF : (half + 1) * HALF, :] = t.astype(BF)
 
+    build_kron(0, 0, CHANNELS)
+    for c in small:
+        c.wait()
     for side in range(2):
-        source_of[side] = srcv[side][...]
 
         def place(j, carry, side=side):
-            slot_at[side, j] = (src[side][j] >> 1) * CHANNELS + chn[side][j]
+            slot_at[side, j] = (lists[side, j] >> 1) * CHANNELS + lists[2 + side, j]
             return carry
 
         lax.fori_loop(0, 2 * SLOTS, place, 0, unroll=8)
-    build_kron(0, 0, CHANNELS)
     local[0].wait()
 
     def before_mix(side, i):
@@ -300,27 +308,21 @@
 
         @at(1, 1)
         def _():
+            gather_step(1, 3)
+
+        @at(1, 2)
+        def _():
+            pass_on(0)
             gather_step(1, 4)
 
-        @at(1, 2)
+        @at(1, 4)
         def _():
             pass_on(1)
-
-        @at(1, 3)
-        def _():
             gather_step(1, 5)
 
-        @at(1, 4)
-        def _():
-            sum_first(0)
-
-        @at(1, 5)
+        @at(1, 6)
         def _():
             gather_step(1, 6)
-
-        @at(1, 7)
-        def _():
-            sum_first(1)
 
         @pl.when(i == 0)
         def _():
@@ -349,7 +351,7 @@
 
         def one_sector(k, carry):
             def during(seg):
-                @pl.when((side == 0) & (k == 0) & (seg == 3))
+                @pl.when((side == 0) & (k == 0) & (seg == 1))
                 def _():
                     gather_step(1, 0)
 
@@ -357,33 +359,36 @@
                 def _():
                     gather_step(1, 1)
 
-                @pl.when((side == 0) & (k == 1) & (seg == 2))
+                @pl.when((side == 1) & (k == 0) & (seg == 0))
                 def _():
-                    gather_step(1, 2)
-
-                @pl.when((side == 1) & (k == 1) & (seg == 3))
-                def _():
-                    pass_on(2)
+                    sum_first(0)
 
             multiply(side, k, during)
 
             def one_half(half, carry):
                 contract(side, k, half)
                 send_first(side * 2 + k, half)
+
+                @pl.when((side == 0) & (k == 1) & (half == 0))
+                def _():
+                    gather_step(1, 2)
+
+                @pl.when((side == 1) & (k == 1) & (half == 0))
+                def _():
+                    pass_on(2)
+
                 return carry
 
             lax.fori_loop(0, 2, one_half, 0)
 
             @pl.when((side == 0) & (k == 1))
             def _():
-                pass_on(0)
-                gather_step(1, 3)
                 local[3].wait()
                 build_rows(1)
 
             @pl.when((side == 1) & (k == 0))
             def _():
-                sum_second(0)
+                sum_first(1)
 
             return carry
 
@@ -391,8 +396,9 @@
         return carry
 
     lax.fori_loop(0, 2, one_side, 0)
+    sum_second(0)
+    sum_second(1)
     pass_on(3)
-    sum_second(1)
     sum_first(2)
     sum_first(3)
     sum_second(2)
@@ -401,7 +407,8 @@
     for side in range(2):
         for n in range(LAST + 1):
             for way in range(2):
-                ring(side, way, n).wait_send()
+                ring(side, way, n, 0).wait_send()
+                ring(side, way, n, 1).wait_send()
                 cross(side, way, n).wait_send()
         for n in range(2):
             cross(side, 2, n).wait_send()
@@ -411,6 +418,11 @@
                 first_copy(u, half, c).wait_send()
             for d in range(3):
                 second_copy(u, half, d).wait_send()
+
+
+def hand_out(a, b, out_a, out_b):
+    out_a[...] = a[...]
+    out_b[...] = b[...]
 
 
 def per_device(
@@ -424,7 +436,7 @@
     new_left, new_right = pl.pallas_call(
         kernel,
         out_shape=[jax.ShapeDtypeStruct((2, WR, S), BF)] * 2,
-        in_specs=[smem] * 6 + [vmem] * 4 + [hbm] * 4,
+        in_specs=[smem] * 2 + [hbm] * 6 + [vmem] * 2 + [hbm] * 4,
         out_specs=[vmem, vmem],
         scratch_shapes=[
             pltpu.VMEM((2, 2 * NZ, 2, WR, S), BF),
@@ -437,11 +449,12 @@
             pltpu.VMEM((4, 2, 6, 2, HALF, S), BF),
             pltpu.VMEM((4, 2, 4, HALF, S), BF),
             pltpu.VMEM((4, 2, 3, HALF, S), BF),
+            pltpu.SMEM((4, 2 * SLOTS), jnp.int32),
             pltpu.SMEM((2, 2 * SLOTS), jnp.int32),
             pltpu.VMEM((2, 1, 2 * SLOTS), jnp.int32),
-            dma((4,)),
-            dma((2, 2, LAST + 1)),
-            dma((2, 2, LAST + 1)),
+            dma((10,)),
+            dma((2, 2, LAST + 1, 2)),
+            dma((2, 2, LAST + 1, 2)),
             dma((2, 2 * NZ)),
             dma((2, 2 * NZ)),
             dma((4, 2, 6)),
@@ -457,6 +470,12 @@
         source_left.reshape(1, -1), source_right.reshape(1, -1), operator_table, operator_pattern,
         env_left.reshape(2, WR, S), env_right.reshape(2, WR, S), site_left, site_right,
     )
+    new_left, new_right = pl.pallas_call(
+        hand_out,
+        out_shape=[jax.ShapeDtypeStruct((2, WR, S), BF)] * 2,
+        in_specs=[vmem, vmem],
+        out_specs=[vmem, vmem],
+    )(new_left, new_right)
     return new_left.reshape(2, W, R, S), new_right.reshape(2, W, R, S)
 
 

time: 81.9 us -> 80.2 us (0.979)
  local copies, waits for them, and re-layouts: 3.19 us -> 0 us
  Pallas kernels: 76.5 us -> 78.7 us
    unnamed x2 -> x0, local copies, waits for them, and re-layouts: 3.19 us -> none
    pallas_call x0 -> x1, Pallas kernels: none -> 1.73 us  [per_device(): pl.pallas_call(hand_out, out_shape=[jax.ShapeDtypeStruct((2, WR, S), BF)]...]
where the time goes in v4:
time: 80.2 us; the launch traced here: 79.3 us
  Pallas kernels  78.7 us (98%)
    pallas_call x1, Pallas kernels, per_device(): pl.pallas_call(kernel, out_shape=[jax.ShapeDtypeStruct((2, WR, S), BF)] *...  76.9 us
    pallas_call x1, Pallas kernels, per_device(): pl.pallas_call(hand_out, out_shape=[jax.ShapeDtypeStruct((2, WR, S), BF)]...  1.73 us

profile of v4, /device:TPU:1, one launch (start us, length us, event | category | flops | bytes accessed | tf_op | source)
XLA Modules:
  0.0 79.3 jit_solution(9495655353330127032)
XLA Ops:
  0.6 76.9 %shard_map.131 = (bf16[2,320,128]{2,1,0:T(8,128)(2,1)}, bf16[2,320,128]{2,1,0:T(8,128)(2,1)}) custom-call(s32[2]{0:T(128)} %fan_l.1, s32[2]{0:T(128)} %fan_r.1, s32[128]{0:T(128)} %src_l.1, s32[128]{0:T(128)} %src_r.1, s32[128]{0:T(128)} %chn_l.1, s32[128]{0:T(128)} %chn_r.1, s32[1,128]{1,0:T(1,128)} %bitcast.8, s32[1,128]{1,0:T(1,128)} %bitcast.9, ...), custom_call_target="tpu_custom_call" | custom-call | tf_op jit(solution)/shard_map/pallas_call | solution.py:436
  77.6 1.7 %shard_map.132 = (bf16[2,320,128]{2,1,0:T(8,128)(2,1)}, bf16[2,320,128]{2,1,0:T(8,128)(2,1)}) custom-call(bf16[2,320,128]{2,1,0:T(8,128)(2,1)} %get-tuple-element.6.a, bf16[2,320,128]{2,1,0:T(8,128)(2,1)} %get-tuple-element.7.b), custom_call_target="tpu_custom_call" | custom-call | tf_op jit(solution)/shard_map/pallas_call | solution.py:473

commit v5 on v4

--- a/solution.py
+++ b/solution.py
@@ -42,6 +42,16 @@
     partners = [other, up, down] + x_peer + y_peer
     for peer in partners:
         pl.semaphore_signal(barrier, inc=1, device_id=peer, device_id_type=MESH)
+    local = [
+        pltpu.make_async_copy(env_in[0], got.at[0, sec], loc_sem.at[0]),
+        pltpu.make_async_copy(env_in[1], got.at[1, sec], loc_sem.at[1]),
+        pltpu.make_async_copy(site_in[0], site.at[0], loc_sem.at[2]),
+        pltpu.make_async_copy(site_in[1], site.at[1], loc_sem.at[3]),
+    ]
+    small = [pltpu.make_async_copy(a, lists.at[i], loc_sem.at[4 + i]) for i, a in enumerate((src_l, src_r, chn_l, chn_r))]
+    small += [pltpu.make_async_copy(a, source_of.at[i], loc_sem.at[8 + i]) for i, a in enumerate((srcv_l, srcv_r))]
+    for c in small + local:
+        c.start()
     pl.semaphore_wait(barrier, len(partners))
 
     def remote(a, b, ssem, rsem, peer):
@@ -108,17 +118,7 @@
         for way in range(2):
             cross_in(side, way, n).wait_recv()
 
-    local = [
-        pltpu.make_async_copy(env_in[0], got.at[0, sec], loc_sem.at[0]),
-        pltpu.make_async_copy(env_in[1], got.at[1, sec], loc_sem.at[1]),
-        pltpu.make_async_copy(site_in[0], site.at[0], loc_sem.at[2]),
-        pltpu.make_async_copy(site_in[1], site.at[1], loc_sem.at[3]),
-    ]
-    small = [pltpu.make_async_copy(a, lists.at[i], loc_sem.at[4 + i]) for i, a in enumerate((src_l, src_r, chn_l, chn_r))]
-    small += [pltpu.make_async_copy(a, source_of.at[i], loc_sem.at[8 + i]) for i, a in enumerate((srcv_l, srcv_r))]
     gather_start(0)
-    for c in small + local:
-        c.start()
 
     spread = (lax.broadcasted_iota(jnp.int32, (WR, W), 0) >> 3 == lax.broadcasted_iota(jnp.int32, (WR, W), 1))
     spread = spread.astype(F32).astype(BF)
@@ -294,13 +294,13 @@
         @at(0, 5)
         def _():
             gather_step(0, 4)
+            gather_step(0, 5)
+
+        @at(0, 7)
+        def _():
+            gather_step(0, 6)
+            gather_start(1)
             build_kron(1, 0, CHANNELS)
-            gather_step(0, 5)
-            gather_start(1)
-
-        @at(0, 7)
-        def _():
-            gather_step(0, 6)
 
         @at(1, 0)
         def _():
@@ -321,6 +321,10 @@
             gather_step(1, 5)
 
         @at(1, 6)
+        def _():
+            sum_first(0)
+
+        @at(1, 7)
         def _():
             gather_step(1, 6)
 
@@ -359,10 +363,6 @@
                 def _():
                     gather_step(1, 1)
 
-                @pl.when((side == 1) & (k == 0) & (seg == 0))
-                def _():
-                    sum_first(0)
-
             multiply(side, k, during)
 
             def one_half(half, carry):
@@ -396,14 +396,19 @@
         return carry
 
     lax.fori_loop(0, 2, one_side, 0)
+    def sent(units):
+        def body(i, carry):
+            u, half = units + i // 2, i % 2
+            for c in range(6):
+                first_copy(u, half, c).wait_send()
+            for d in range(3):
+                second_copy(u, half, d).wait_send()
+            return carry
+
+        lax.fori_loop(0, 4, body, 0)
+
     sum_second(0)
     sum_second(1)
-    pass_on(3)
-    sum_first(2)
-    sum_first(3)
-    sum_second(2)
-    sum_second(3)
-
     for side in range(2):
         for n in range(LAST + 1):
             for way in range(2):
@@ -412,12 +417,13 @@
                 cross(side, way, n).wait_send()
         for n in range(2):
             cross(side, 2, n).wait_send()
-    for u in range(4):
-        for half in range(2):
-            for c in range(6):
-                first_copy(u, half, c).wait_send()
-            for d in range(3):
-                second_copy(u, half, d).wait_send()
+    sent(0)
+    pass_on(3)
+    sum_first(2)
+    sum_first(3)
+    sum_second(2)
+    sum_second(3)
+    sent(2)
 
 
 def hand_out(a, b, out_a, out_b):

time: 80.2 us -> 79 us (0.985)
  Pallas kernels: 78.7 us -> 77.5 us
    pallas_call x1, Pallas kernels: 76.9 us -> 75.8 us  [per_device(): pl.pallas_call(kernel, out_shape=[jax.ShapeDtypeStruct((2, WR, S), BF)] *...]
where the time goes in v5:
time: 79 us; the launch traced here: 78.2 us
  Pallas kernels  77.5 us (98%)
    pallas_call x1, Pallas kernels, per_device(): pl.pallas_call(kernel, out_shape=[jax.ShapeDtypeStruct((2, WR, S), BF)] *...  75.8 us
    pallas_call x1, Pallas kernels, per_device(): pl.pallas_call(hand_out, out_shape=[jax.ShapeDtypeStruct((2, WR, S), BF)]...  1.73 us

profile of v5, /device:TPU:1, one launch (start us, length us, event | category | flops | bytes accessed | tf_op | source)
XLA Modules:
  0.0 78.2 jit_solution(1787239280215113291)
XLA Ops:
  0.6 75.8 %shard_map.131 = (bf16[2,320,128]{2,1,0:T(8,128)(2,1)}, bf16[2,320,128]{2,1,0:T(8,128)(2,1)}) custom-call(s32[2]{0:T(128)} %fan_l.1, s32[2]{0:T(128)} %fan_r.1, s32[128]{0:T(128)} %src_l.1, s32[128]{0:T(128)} %src_r.1, s32[128]{0:T(128)} %chn_l.1, s32[128]{0:T(128)} %chn_r.1, s32[1,128]{1,0:T(1,128)} %bitcast.8, s32[1,128]{1,0:T(1,128)} %bitcast.9, ...), custom_call_target="tpu_custom_call" | custom-call | tf_op jit(solution)/shard_map/pallas_call | solution.py:442
  76.5 1.7 %shard_map.132 = (bf16[2,320,128]{2,1,0:T(8,128)(2,1)}, bf16[2,320,128]{2,1,0:T(8,128)(2,1)}) custom-call(bf16[2,320,128]{2,1,0:T(8,128)(2,1)} %get-tuple-element.6.a, bf16[2,320,128]{2,1,0:T(8,128)(2,1)} %get-tuple-element.7.b), custom_call_target="tpu_custom_call" | custom-call | tf_op jit(solution)/shard_map/pallas_call | solution.py:479
